TPU v7x, 512 devices: a whole 4x4x16 slice. The times are simulated.
512 devices in a mesh: seq: 64 (over z, y), head: 4 (over x), dp: 2 (over core).
Axes of the slice: x: 4, y: 4, z: 16, core: 2. Of those that a mesh axis runs over, the one named last changes fastest.
Arguments:
- queries: bfloat16 [2, 8192, 4096], P('dp', 'seq', 'head'), may hold values from -0.23925781 to 0.23925781
- key_rows: bfloat16 [2, 8192, 4096], P('dp', 'seq', 'head'), may hold values from -0.23925781 to 0.23925781
- values: bfloat16 [2, 8192, 4096], P('dp', 'seq', 'head'), may hold values from -6 to 6
- out_grad: bfloat16 [2, 8192, 4096], P('dp', 'seq', 'head'), may hold values from -6 to 6
- decay_rate: float32 [32], P('head'), may hold values from 4e-05 to 0.025, as said below
- rotation: float32 [4, 4096], P(None, 'head')
- refusal: float32 [4096, 2], P('head')
- proj_weight: float32 [4, 4096], P(None, 'head'), may hold values from -0.09375 to 0.09375
- proj_bias: float32 [4], replicated, may hold values from -4 to 4
- positions: int32 [2, 16], P('dp'), may hold values from 0 to 8191, as said below
Outputs:
- attended: bfloat16 [2, 8192, 4096], P('dp', 'seq', 'head')
- grad_query: bfloat16 [2, 8192, 4096], P('dp', 'seq', 'head')
- grad_key: bfloat16 [2, 8192, 4096], P('dp', 'seq', 'head')
- grad_value: bfloat16 [2, 8192, 4096], P('dp', 'seq', 'head')
- grad_rotation: float32 [4, 4096], P(None, 'head')
- grad_weight: float32 [4, 4096], P(None, 'head')
- grad_bias: float32 [4], replicated
Inputs may be any that keep to these rules, and one draw needn't show every extreme that they name: 16 distinct positions in ascending order; among them always 0, 4096 and 8191. `decay_rate`: one rate per head, the same at every position.
All inputs are finite; a program needn't handle non-finite values.
Results may differ from a plain program's by a relative error of at most 0.0032.
Values sent between devices are 32-bit elements; how exact they have to be, the bound alone decides.
No kernel may reach another device: no remote copies, remote signals or barrier semaphores. Data moves between devices by JAX's collectives and lax.ppermute only.
A program may use at most 128 MiB of HBM per device.

v0:
```python
import jax
import jax.numpy as jnp
from jax import lax
from jax.sharding import PartitionSpec as P

highest = lax.Precision.HIGHEST


def carried_in(x, axis, combine, identity, reverse):
    peers, place = (lax.axis_size(axis), lax.axis_index(axis))
    everything = jax.tree.map(lambda part: lax.all_gather(part, axis), x)
    start = jax.tree.map(
        lambda part, zero: jnp.broadcast_to(jnp.asarray(zero, part.dtype), part.shape), x, identity
    )

    def lap(k, before):
        at = peers - 1 - k if reverse else k
        reached = at > place if reverse else at < place
        new = combine(before, jax.tree.map(lambda part: part[at], everything))
        return jax.tree.map(lambda a, b: jnp.where(reached, a, b), new, before)

    return lax.fori_loop(0, peers, lap, start)


def decay_table(log_decay, count):
    offsets = jnp.arange(count)
    between = offsets[:, None] - offsets[None, :]
    powers = jnp.exp(jnp.maximum(between, 0).astype(jnp.float32)[None] * log_decay[:, None, None])
    return jnp.where(between[None] >= 0, powers, 0.0)


def gram_inverse(gram):
    determinant = gram[0, 0] * gram[1, 1] - gram[0, 1] * gram[1, 0]
    adjugate = jnp.stack(
        [jnp.stack([gram[1, 1], -gram[0, 1]]), jnp.stack([-gram[1, 0], gram[0, 0]])]
    )
    return adjugate / determinant


def chain_combine(earlier, later):
    return (earlier[0] * later[0], later[0][:, None, None] * earlier[1] + later[1])


def shards(
    queries,
    key_rows,
    values,
    out_grad,
    decay_rate,
    rotation,
    refusal,
    proj_weight,
    proj_bias,
    positions,
):
    group = queries.shape[1]
    local_width = queries.shape[2]
    local_heads = decay_rate.shape[0]
    head_size = local_width // local_heads
    query_heads = queries[0].reshape(group, local_heads, head_size)
    key_heads = key_rows[0].reshape(group, local_heads, head_size)
    grad_heads = out_grad[0].reshape(group, local_heads, head_size)
    places = lax.axis_index("seq") * group + jnp.arange(group, dtype=jnp.int32)
    selector = places[:, None] == positions[0][None, :]
    select_low = selector.astype(jnp.bfloat16)
    select_full = selector.astype(jnp.float32)
    picked = jnp.dot(select_low.T, values[0], preferred_element_type=jnp.float32)
    gram_part = jnp.dot(refusal.T, refusal, precision=highest)
    coupling_part = jnp.dot(rotation, refusal, precision=highest)
    gram, coupling = lax.psum((gram_part, coupling_part), "head")
    inverse = gram_inverse(gram)
    rotated = rotation - jnp.dot(
        jnp.dot(coupling, inverse, precision=highest), refusal.T, precision=highest
    )
    code = (
        lax.psum(jnp.dot(picked, (proj_weight - rotated).T, precision=highest), "head") + proj_bias
    )
    shift_rows = jnp.dot(code, rotated, precision=highest)
    moved = (
        values[0].astype(jnp.float32) + jnp.dot(select_full, shift_rows, precision=highest)
    ).astype(jnp.bfloat16)
    moved_heads = moved.reshape(group, local_heads, head_size)
    log_decay = jnp.log1p(-decay_rate)
    table = decay_table(log_decay, group)
    offsets = jnp.arange(group).astype(jnp.float32)
    enter = jnp.exp((offsets + 1.0)[:, None] * log_decay[None, :])
    leave = jnp.exp((group - offsets)[:, None] * log_decay[None, :])
    start_weight = jnp.exp(offsets[:, None] * log_decay[None, :])
    end_weight = jnp.exp((group - 1.0 - offsets)[:, None] * log_decay[None, :])
    keep = jnp.exp(group * log_decay)
    query_full = query_heads.astype(jnp.float32)
    key_full = key_heads.astype(jnp.float32)
    moved_full = moved_heads.astype(jnp.float32)
    grad_full = grad_heads.astype(jnp.float32)
    local_state = jnp.einsum(
        "shd,she->hde", key_full * end_weight[:, :, None], moved_full, precision=highest
    )
    local_grad = jnp.einsum(
        "thd,the->hde", query_full * start_weight[:, :, None], grad_full, precision=highest
    )
    blank = (jnp.ones_like(keep), jnp.zeros_like(local_state))
    entering = carried_in((keep, local_state), "seq", chain_combine, blank, False)[1]
    leaving = carried_in((keep, local_grad), "seq", chain_combine, blank, True)[1]
    scores = jnp.einsum("thd,shd->hts", query_heads, key_heads, preferred_element_type=jnp.float32)
    mixing = (scores * table).astype(jnp.bfloat16)
    inner = jnp.einsum("hts,she->the", mixing, moved_heads, preferred_element_type=jnp.float32)
    outer = enter[:, :, None] * jnp.einsum("thd,hde->the", query_full, entering, precision=highest)
    attended = (inner + outer).astype(jnp.bfloat16).reshape(1, group, local_width)
    grad_scores = jnp.einsum(
        "the,she->hts", grad_heads, moved_heads, preferred_element_type=jnp.float32
    )
    grad_mixing = (grad_scores * table).astype(jnp.bfloat16)
    grad_query = jnp.einsum(
        "hts,shd->thd", grad_mixing, key_heads, preferred_element_type=jnp.float32
    )
    grad_query = grad_query + enter[:, :, None] * jnp.einsum(
        "the,hde->thd", grad_full, entering, precision=highest
    )
    grad_key = jnp.einsum(
        "hts,thd->shd", grad_mixing, query_heads, preferred_element_type=jnp.float32
    )
    grad_key = grad_key + leave[:, :, None] * jnp.einsum(
        "she,hde->shd", moved_full, leaving, precision=highest
    )
    grad_moved = jnp.einsum("hts,the->she", mixing, grad_heads, preferred_element_type=jnp.float32)
    grad_moved = grad_moved + leave[:, :, None] * jnp.einsum(
        "shd,hde->she", key_full, leaving, precision=highest
    )
    grad_moved = grad_moved.reshape(group, local_width)
    picked_grad = jnp.dot(select_full.T, grad_moved, precision=highest)
    code_grad = lax.psum(jnp.dot(picked_grad, rotated.T, precision=highest), "head")
    rotated_grad = jnp.dot(code.T, picked_grad, precision=highest) - jnp.dot(
        code_grad.T, picked, precision=highest
    )
    projected = lax.psum(jnp.dot(rotated_grad, refusal, precision=highest), "head")
    rotation_part = rotated_grad - jnp.dot(
        jnp.dot(projected, inverse, precision=highest), refusal.T, precision=highest
    )
    weight_part = jnp.dot(code_grad.T, picked, precision=highest)
    bias_part = jnp.sum(code_grad, axis=0)
    grad_weight, grad_bias, grad_rotation = lax.psum(
        (weight_part, bias_part, rotation_part), ("seq", "dp")
    )
    value_fix = jnp.dot(code_grad, proj_weight - rotated, precision=highest)
    grad_value = (
        (grad_moved + jnp.dot(select_full, value_fix, precision=highest))
        .astype(jnp.bfloat16)
        .reshape(1, group, local_width)
    )
    grad_query = grad_query.astype(jnp.bfloat16).reshape(1, group, local_width)
    grad_key = grad_key.astype(jnp.bfloat16).reshape(1, group, local_width)
    return (attended, grad_query, grad_key, grad_value, grad_rotation, grad_weight, grad_bias)


def solution(mesh):
    return jax.shard_map(
        shards,
        mesh=mesh,
        in_specs=(
            P("dp", "seq", "head"),
            P("dp", "seq", "head"),
            P("dp", "seq", "head"),
            P("dp", "seq", "head"),
            P("head"),
            P(None, "head"),
            P("head", None),
            P(None, "head"),
            P(),
            P("dp", None),
        ),
        out_specs=(
            P("dp", "seq", "head"),
            P("dp", "seq", "head"),
            P("dp", "seq", "head"),
            P("dp", "seq", "head"),
            P(None, "head"),
            P(None, "head"),
            P(),
        ),
        check_vma=False,
    )
```

profile of v0, /device:TPU:2, one launch (start us, length us, event | category | flops | bytes accessed | tf_op | source)
XLA Modules:
  0.0 1008.6 jit_solution(10857134564750874823)
XLA Ops:
  9.5 1.3 dynamic-slice
  12.3 1.5 fusion.20
  14.9 13.6 %all-reduce.3 = (f32[4,2]{0,1:T(2,128)S(1)}, f32[2,2]{1,0:T(2,128)S(1)}) all-reduce(f32[4,2]{0,1:T(2,128)S(1)} %fusion.63, f32[2,2]{1,0:T(2,128)S(1)} %fusion.64), channel_id=1, replica_groups=mesh['seq'=64,'head'=4,'dp'=2] {'head'}, use_global_device_ids=true, to_apply=%region_0.0 | all-reduce | flops 12 | bytes 96 | tf_op jit(solution)/shard_map/psum | solution.py:70
  31.7 146.4 %all-reduce = f32[512]{0:T(512)S(1)} all-reduce(f32[512]{0:T(512)S(1)} %get-tuple-element.328), channel_id=2, replica_groups=mesh['seq'=64,'head'=4,'dp'=2] {'seq'}, use_global_device_ids=true, to_apply=%add | all-reduce | flops 512 | bytes 4096
  180.8 1.4 maximum_bitcast_fusion
  183.9 1.2 fusion.30
  186.4 127.3 %all-gather.8.cloned.1.call-done = f32[512,128,128]{2,1,0:T(8,128)} async-done(((f32[8,128,128]{2,1,0:T(8,128)}), f32[512,128,128]{2,1,0:T(8,128)}) %all-gather.8.cloned.1.call-update) | async-done | bytes 33554448 | tf_op jit(solution)/shard_map/all_gather | solution.py:11
  313.7 78.5 %while.31 = (s32[]{:T(128)}, f32[8,128,128]{2,1,0:T(8,128)S(1)}, s32[]{:T(128)}, f32[64,8]{1,0:T(8,128)S(1)}, f32[64,8,128,128]{3,2,1,0:T(8,128)}, /*index=5*/s32[]{:T(128)}, s32[]{:T(128)}, s32[]{:T(128)}, s32[]{:T(128)}) while((s32[]{:T(128)}, f32[8,128,128]{2,1,0:T(8,128)S(1)}, s32[]{:T(128)}, f32[64,8]{1,0:T(8,128)S(1)}, ...), condition=%wide.region_6.7_spmd.clone, body=%wide.region_5.6_spmd.clone.sunk | while | flops 524296 | bytes 1573127 | solution.py:22
  318.6 1.2 fusion.114
  324.7 1.2 fusion.114
  333.3 1.2 fusion.114
  341.9 1.2 fusion.114
  348.1 1.2 fusion.114
  356.6 1.2 fusion.114
  365.2 1.2 fusion.114
  371.4 1.2 fusion.114
  394.3 8.6 all-reduce.2
  403.9 1.4 fusion.19
  405.3 1.2 fusion.23
  407.7 10.2 %psum.60 = f32[4,2]{0,1:T(2,128)S(1)} all-reduce(f32[4,2]{0,1:T(2,128)S(1)} %fusion.68), channel_id=1, replica_groups=mesh['seq'=64,'head'=4,'dp'=2] {'head'}, use_global_device_ids=true, to_apply=%region_8.9 | all-reduce | flops 8 | bytes 64 | tf_op jit(solution)/shard_map/psum | solution.py:135
  418.2 1.2 fusion.16
  422.3 495.7 %all-reduce.1 = (f32[4,1024]{1,0:T(4,128)}, f32[4,1024]{1,0:T(4,128)}, f32[4]{0:T(128)}) all-reduce(f32[4,1024]{1,0:T(4,128)S(1)} %convolution_subtract_fusion, f32[4,1024]{1,0:T(4,128)S(1)} %fusion.67, f32[4]{0:T(128)S(1)} %reduce_sum.9), channel_id=1, replica_groups=mesh['seq'=64,'head'=4,'dp'=2] {'seq','dp'}, use_global_device_ids=true, to_apply=%region_9.10 | all-reduce | flops 8196 | bytes 65568 | tf_op jit(solution)/shard_map/psum | solution.py:141
  919.0 1.8 fusion.18
  920.8 77.7 %while.30 = (s32[]{:T(128)}, f32[8,128,128]{2,1,0:T(8,128)S(1)}, s32[]{:T(128)}, f32[64,8]{1,0:T(8,128)S(1)}, f32[64,8,128,128]{3,2,1,0:T(8,128)}, /*index=5*/s32[]{:T(128)}, s32[]{:T(128)}) while((s32[]{:T(128)}, f32[8,128,128]{2,1,0:T(8,128)S(1)}, s32[]{:T(128)}, f32[64,8]{1,0:T(8,128)S(1)}, f32[64,8,128,128]{3,2,1,0:T(8,128)}, ...), condition=%wide.region_4.5_spmd.clone, body=%wide.region_3.4_spmd.clone.sunk | while | flops 524292 | bytes 1573065 | solution.py:22
  (313 shorter events, 162.9 us)
Async XLA Ops:
  7.2 6.7 copy-start
  7.2 306.5 %all-gather.8.cloned.1.call-start = ((), (), s32[]{:S(2)}) async-start(), calls=%async_computation.1 | async-start | bytes 34078720 | tf_op jit(solution)/shard_map/all_gather | solution.py:11
  12.2 301.5 %copy-start.5 = (f32[8]{0:T(128)}, f32[8]{0:T(128)S(1)}, u32[]{:S(2)}) copy-start(f32[8]{0:T(128)S(1)} %get-tuple-element.327) | copy-start | bytes 100
  13.8 907.0 %all-gather.6.cloned.1.call-start = ((), (), s32[]{:S(2)}) async-start(), calls=%async_computation | async-start | bytes 34078720 | tf_op jit(solution)/shard_map/all_gather | solution.py:11
  180.8 237.1 %copy-start.4 = (s32[128]{0:T(128)}, s32[128]{0:T(128)S(1)}, u32[]{:S(2)}) copy-start(s32[128]{0:T(128)S(1)} %iota_add_fusion) | copy-start | bytes 1540
  182.1 0.6 copy-start.6
  182.2 235.7 %copy-start.3 = (pred[128,128]{1,0:T(8,128)(4,1)}, pred[128,128]{1,0:T(8,128)(4,1)S(1)}, u32[]{:S(2)}) copy-start(pred[128,128]{1,0:T(8,128)(4,1)S(1)} %fusion.43) | copy-start | bytes 49156
  182.2 3.8 copy-start.1
  402.9 15.0 %copy-start.2 = (f32[16,4]{0,1:T(4,128)}, f32[16,4]{0,1:T(4,128)S(1)}, u32[]{:S(2)}) copy-start(f32[16,4]{0,1:T(4,128)S(1)} %get-tuple-element.316) | copy-start | bytes 772
Sparse Core Ops, SparseCore 0:
  13.9 299.7 all-gather.7
  406.6 291.8 all-gather.5
where the time goes:
time: 1020 us; the launch traced here: 1010 us
  blocking collectives  674 us (66%)
  other arithmetic  153 us (15%)
  waiting for transfers between devices  127 us (12%)
  matrix products  20.5 us (2%)
  between operations  18.9 us (2%)
    psum x1, blocking collectives, shards(): lax.psum((weight_part, bias_part, rotation_part), ('seq', 'dp'))  496 us
    select_n x128, other arithmetic, lap(): return jax.tree.map(lambda a, b: jnp.where(reached, a, b), new, before)  150 us
    unnamed x1, blocking collectives  146 us
    all_gather x2, waiting for transfers between devices, carried_in(): everything = jax.tree.map(lambda part: lax.all_gather(part, axis), x)  127 us
  transfers between devices with their start and end apart: 2, of which 1 were waited for; matrix products, arithmetic and copies ran while one was open for 2% of the time, Pallas kernels for 0%

commit v1 on v0

--- a/solution.py
+++ b/solution.py
@@ -138,9 +138,8 @@
     )
     weight_part = jnp.dot(code_grad.T, picked, precision=highest)
     bias_part = jnp.sum(code_grad, axis=0)
-    grad_weight, grad_bias, grad_rotation = lax.psum(
-        (weight_part, bias_part, rotation_part), ("seq", "dp")
-    )
+    run_page = lambda patch: lax.psum(lax.psum(patch, "seq"), "dp")
+    grad_weight, grad_bias, grad_rotation = run_page((weight_part, bias_part, rotation_part))
     value_fix = jnp.dot(code_grad, proj_weight - rotated, precision=highest)
     grad_value = (
         (grad_moved + jnp.dot(select_full, value_fix, precision=highest))

time: 1020 us -> 804 us (0.79)
  the two profiles are of different devices: /device:TPU:2 before, /device:TPU:1 now
where the time goes in v1:
time: 804 us; the launch traced here: 797 us
  blocking collectives  435 us (54%)
  waiting for transfers between devices  155 us (19%)
  other arithmetic  153 us (19%)
  matrix products  20.6 us (3%)
  between operations  18.9 us (2%)
  local copies, waits for them, and re-layouts  9.93 us (1%)
    psum x2, blocking collectives, shards(): run_page = lambda patch: lax.psum(lax.psum(patch, 'seq'), 'dp')  288 us
    all_gather x2, waiting for transfers between devices, carried_in(): everything = jax.tree.map(lambda part: lax.all_gather(part, axis), x)  155 us
    select_n x128, other arithmetic, lap(): return jax.tree.map(lambda a, b: jnp.where(reached, a, b), new, before)  150 us
    unnamed x1, blocking collectives  124 us
  transfers between devices with their start and end apart: 2, of which 1 were waited for; matrix products, arithmetic and copies ran while one was open for 2% of the time, Pallas kernels for 0%

profile of v1, /device:TPU:1, one launch (start us, length us, event | category | flops | bytes accessed | tf_op | source)
XLA Modules:
  0.0 797.1 jit_solution(4369469670726650017)
XLA Ops:
  9.5 1.3 dynamic-slice
  12.3 1.5 fusion.20
  14.9 9.3 %all-reduce.3 = (f32[4,2]{0,1:T(2,128)S(1)}, f32[2,2]{1,0:T(2,128)S(1)}) all-reduce(f32[4,2]{0,1:T(2,128)S(1)} %fusion.63, f32[2,2]{1,0:T(2,128)S(1)} %fusion.64), channel_id=1, replica_groups=mesh['seq'=64,'head'=4,'dp'=2] {'head'}, use_global_device_ids=true, to_apply=%region_0.0 | all-reduce | flops 12 | bytes 96 | tf_op jit(solution)/shard_map/psum | solution.py:70
  27.4 123.5 %all-reduce = f32[512]{0:T(512)S(1)} all-reduce(f32[512]{0:T(512)S(1)} %get-tuple-element.331), channel_id=2, replica_groups=mesh['seq'=64,'head'=4,'dp'=2] {'seq'}, use_global_device_ids=true, to_apply=%add | all-reduce | flops 512 | bytes 4096
  153.6 1.4 maximum_bitcast_fusion
  156.7 1.2 fusion.30
  159.2 154.9 %all-gather.8.cloned.1.call-done = f32[512,128,128]{2,1,0:T(8,128)} async-done(((f32[8,128,128]{2,1,0:T(8,128)}), f32[512,128,128]{2,1,0:T(8,128)}) %all-gather.8.cloned.1.call-update) | async-done | bytes 33554448 | tf_op jit(solution)/shard_map/all_gather | solution.py:11
  314.1 78.5 %while.31 = (s32[]{:T(128)}, f32[8,128,128]{2,1,0:T(8,128)S(1)}, s32[]{:T(128)}, f32[64,8]{1,0:T(8,128)S(1)}, f32[64,8,128,128]{3,2,1,0:T(8,128)}, /*index=5*/s32[]{:T(128)}, s32[]{:T(128)}, s32[]{:T(128)}, s32[]{:T(128)}) while((s32[]{:T(128)}, f32[8,128,128]{2,1,0:T(8,128)S(1)}, s32[]{:T(128)}, f32[64,8]{1,0:T(8,128)S(1)}, ...), condition=%wide.region_6.7_spmd.clone, body=%wide.region_5.6_spmd.clone.sunk | while | flops 524296 | bytes 1573127 | solution.py:22
  316.5 1.2 fusion.114
  322.7 1.2 fusion.114
  331.3 1.2 fusion.114
  339.9 1.2 fusion.114
  346.0 1.2 fusion.114
  354.6 1.2 fusion.114
  363.2 1.2 fusion.114
  394.7 8.5 %all-reduce.2 = (f32[16,4]{0,1:T(4,128)S(1)}, f32[16,4]{0,1:T(4,128)S(1)}) all-reduce(f32[16,4]{0,1:T(4,128)S(1)} %fusion.55, f32[16,4]{0,1:T(4,128)S(1)} %fusion.66), channel_id=1, replica_groups=mesh['seq'=64,'head'=4,'dp'=2] {'head'}, use_global_device_ids=true, to_apply=%region_2.0 | all-reduce | flops 128 | bytes 1024 | tf_op jit(solution)/shard_map/psum | solution.py:76
  404.2 1.4 fusion.19
  405.6 1.2 fusion.23
  408.0 6.0 psum.81
  414.4 1.2 fusion.16
  418.4 223.7 %all-reduce.1 = (f32[4,1024]{1,0:T(4,128)S(1)}, f32[4,1024]{1,0:T(4,128)S(1)}, f32[4]{0:T(128)S(1)}) all-reduce(f32[4,1024]{1,0:T(4,128)S(1)} %convolution_subtract_fusion, f32[4,1024]{1,0:T(4,128)S(1)} %fusion.67, f32[4]{0:T(128)S(1)} %reduce_sum.9), channel_id=1, replica_groups=mesh['seq'=64,'head'=4,'dp'=2] {'seq'}, use_global_device_ids=true, to_apply=%region_9.10 | all-reduce | flops 8196 | bytes 65568 | tf_op jit(solution)/shard_map/psum | solution.py:141
  642.1 64.2 %all-reduce.4 = (f32[4,1024]{1,0:T(4,128)}, f32[4,1024]{1,0:T(4,128)}, f32[4]{0:T(128)}) all-reduce(f32[4,1024]{1,0:T(4,128)S(1)} %get-tuple-element.312, f32[4,1024]{1,0:T(4,128)S(1)} %get-tuple-element.313, f32[4]{0:T(128)S(1)} %get-tuple-element.314), channel_id=1, replica_groups=mesh['seq'=64,'head'=4,'dp'=2] {'dp'}, use_global_device_ids=true, to_apply=%region_10.11 | all-reduce | flops 8196 | bytes 65568 | tf_op jit(solution)/shard_map/psum | solution.py:141
  707.4 1.8 fusion.18
  709.2 77.7 %while.30 = (s32[]{:T(128)}, f32[8,128,128]{2,1,0:T(8,128)S(1)}, s32[]{:T(128)}, f32[64,8]{1,0:T(8,128)S(1)}, f32[64,8,128,128]{3,2,1,0:T(8,128)}, /*index=5*/s32[]{:T(128)}, s32[]{:T(128)}) while((s32[]{:T(128)}, f32[8,128,128]{2,1,0:T(8,128)S(1)}, s32[]{:T(128)}, f32[64,8]{1,0:T(8,128)S(1)}, f32[64,8,128,128]{3,2,1,0:T(8,128)}, ...), condition=%wide.region_4.5_spmd.clone, body=%wide.region_3.4_spmd.clone.sunk | while | flops 524292 | bytes 1573065 | solution.py:22
  (314 shorter events, 164.1 us)
Async XLA Ops:
  7.2 6.7 copy-start
  7.2 306.9 %all-gather.8.cloned.1.call-start = ((), (), s32[]{:S(2)}) async-start(), calls=%async_computation.1 | async-start | bytes 34078720 | tf_op jit(solution)/shard_map/all_gather | solution.py:11
  12.2 301.9 %copy-start.5 = (f32[8]{0:T(128)}, f32[8]{0:T(128)S(1)}, u32[]{:S(2)}) copy-start(f32[8]{0:T(128)S(1)} %get-tuple-element.330) | copy-start | bytes 100
  13.8 695.4 %all-gather.6.cloned.1.call-start = ((), (), s32[]{:S(2)}) async-start(), calls=%async_computation | async-start | bytes 34078720 | tf_op jit(solution)/shard_map/all_gather | solution.py:11
  153.6 260.5 %copy-start.4 = (s32[128]{0:T(128)}, s32[128]{0:T(128)S(1)}, u32[]{:S(2)}) copy-start(s32[128]{0:T(128)S(1)} %iota_add_fusion) | copy-start | bytes 1540
  155.0 0.6 copy-start.6
  155.0 259.0 %copy-start.3 = (pred[128,128]{1,0:T(8,128)(4,1)}, pred[128,128]{1,0:T(8,128)(4,1)S(1)}, u32[]{:S(2)}) copy-start(pred[128,128]{1,0:T(8,128)(4,1)S(1)} %fusion.43) | copy-start | bytes 49156
  155.0 3.8 copy-start.1
  403.2 10.9 %copy-start.2 = (f32[16,4]{0,1:T(4,128)}, f32[16,4]{0,1:T(4,128)S(1)}, u32[]{:S(2)}) copy-start(f32[16,4]{0,1:T(4,128)S(1)} %get-tuple-element.316) | copy-start | bytes 772
Sparse Core Ops, SparseCore 0:
  13.9 300.1 all-gather.7
  406.9 293.5 all-gather.5
